TPU v7x, 128 devices: a whole 4x4x4 slice. The times are simulated.
128 devices in a mesh: img: 8 (over z, x_lo), txt: 16 (over x_hi, y, core).
Axes of the slice: x: 4 (x_hi: 2, x_lo: 2; x = x_hi * 2 + x_lo), y: 4, z: 4, core: 2. Of those that a mesh axis runs over, the one named last changes fastest.
Arguments:
- image_feat: bfloat16 [16384, 1152], P(('img', 'txt')), may hold values from -6 to 6
- text_feat: bfloat16 [16384, 1152], P(('img', 'txt')), may hold values from -6 to 6
- image_head: bfloat16 [1152, 1152], replicated, may hold values from -0.1875 to 0.1875
- text_head: bfloat16 [1152, 1152], replicated, may hold values from -0.1875 to 0.1875
- group_bias: float32 [32], replicated, may hold values from -6 to -4
- text_lang: int32 [16384], P(('img', 'txt')), may hold values from 0 to 31
- partner: int32 [16384], P(('img', 'txt')), may hold values from 0 to 16383, each once
Outputs:
- image_grad: float32 [16384, 1152], P(('img', 'txt'))
- text_grad: float32 [16384, 1152], P(('img', 'txt'))
- image_head_grad: float32 [1152, 1152], P(('img', 'txt'))
- text_head_grad: float32 [1152, 1152], P(('img', 'txt'))
Inputs may be any that keep to these rules, and one draw needn't show every extreme that they name: partner names every image exactly once.
All inputs are finite; a program needn't handle non-finite values.
Results may differ from a plain program's by a relative error of at most 0.02.
Values may be sent and summed in bfloat16 or wider, within the bound.
No kernel may reach another device: no remote copies, remote signals or barrier semaphores. Data moves between devices by JAX's collectives and lax.ppermute only.
A program may use at most 128 MiB of HBM per device.

v0:
```python
import jax
import jax.numpy as jnp
from jax import lax
from jax.sharding import PartitionSpec as P

logit_scale = 64.0
epsilon = 1e-06


def passed_along(block, axis, distance):
    devices = range(lax.axis_size(axis))
    route = [((i - distance) % len(devices), i) for i in devices]
    return lax.ppermute(block, axis, route)


def unit_rows(features, head):
    projected = jnp.dot(features, head, preferred_element_type=jnp.float32)
    row_norm = jnp.sqrt(jnp.sum(projected * projected, axis=1, keepdims=True) + epsilon)
    return (projected, row_norm, (projected / row_norm).astype(jnp.bfloat16))


def back_norm(projected, row_norm, upstream):
    inner = jnp.sum(projected * upstream, axis=1, keepdims=True) / (row_norm * row_norm)
    return ((upstream - projected * inner) / row_norm).astype(jnp.bfloat16)


def pair_tile(images, image_ids, panel_rows, panel_bias, panel_partner):
    scores = (
        logit_scale
        * lax.dot_general(
            images, panel_rows, (((1,), (1,)), ((), ())), preferred_element_type=jnp.float32
        )
        + panel_bias[None, :]
    )
    positive = (panel_partner[None, :] == image_ids[:, None]).astype(jnp.float32)
    slopes = (jax.nn.sigmoid(scores) - positive).astype(jnp.bfloat16)
    image_term = logit_scale * jnp.dot(slopes, panel_rows, preferred_element_type=jnp.float32)
    text_term = logit_scale * lax.dot_general(
        slopes, images, (((0,), (0,)), ((), ())), preferred_element_type=jnp.float32
    )
    return (image_term, text_term)


def shards(image_feat, text_feat, image_head, text_head, group_bias, text_lang, partner):
    row_count, feat_width = image_feat.shape
    img_devices = lax.axis_size("img")
    txt_devices = lax.axis_size("txt")
    txt_place = lax.axis_index("txt")
    proj_img, norm_img, unit_img = unit_rows(image_feat, image_head)
    proj_txt, norm_txt, unit_txt = unit_rows(text_feat, text_head)
    groups = group_bias.shape[0]
    is_group = text_lang[:, None] == jnp.arange(groups, dtype=jnp.int32)[None, :]
    text_bias = jnp.sum(jnp.where(is_group, group_bias[None, :], 0.0), axis=1)
    partner_float = partner.astype(jnp.float32)
    images = lax.all_gather(unit_img, "img", axis=0, tiled=True)
    gathered_index = jnp.arange(img_devices * row_count, dtype=jnp.int32)
    image_ids = (
        (gathered_index // row_count * txt_devices + txt_place) * row_count
        + gathered_index % row_count
    ).astype(jnp.float32)
    image_zero = jnp.zeros((img_devices * row_count, feat_width), jnp.float32)

    def cycle_turn(turn_index, cycle_state):
        panel_rows, grad_rows, panel_bias, panel_partner, image_acc = cycle_state
        image_term, text_term = pair_tile(images, image_ids, panel_rows, panel_bias, panel_partner)
        panel_rows = passed_along(panel_rows, "txt", 1)
        grad_rows, panel_bias, panel_partner = passed_along(
            (grad_rows + text_term, panel_bias, panel_partner), "txt", 1
        )
        return (panel_rows, grad_rows, panel_bias, panel_partner, image_acc + image_term)

    start_state = (
        unit_txt,
        jnp.zeros((row_count, feat_width), jnp.float32),
        text_bias,
        partner_float,
        image_zero,
    )
    cycle_state = lax.fori_loop(0, txt_devices, cycle_turn, start_state)
    text_up = cycle_state[1]
    image_acc = cycle_state[4]
    image_up = lax.psum_scatter(
        image_acc.astype(jnp.bfloat16), "img", scatter_dimension=0, tiled=True
    ).astype(jnp.float32)
    grad_img = back_norm(proj_img, norm_img, image_up)
    grad_txt = back_norm(proj_txt, norm_txt, text_up)
    image_grad = lax.dot_general(
        grad_img, image_head, (((1,), (1,)), ((), ())), preferred_element_type=jnp.float32
    )
    text_grad = lax.dot_general(
        grad_txt, text_head, (((1,), (1,)), ((), ())), preferred_element_type=jnp.float32
    )
    image_part = lax.dot_general(
        image_feat, grad_img, (((0,), (0,)), ((), ())), preferred_element_type=jnp.float32
    )
    text_part = lax.dot_general(
        text_feat, grad_txt, (((0,), (0,)), ((), ())), preferred_element_type=jnp.float32
    )
    head_terms = lax.psum_scatter(
        jnp.concatenate([image_part, text_part], axis=1),
        ("img", "txt"),
        scatter_dimension=0,
        tiled=True,
    )
    return (image_grad, text_grad, head_terms[:, :feat_width], head_terms[:, feat_width:])


def solution(mesh):
    in_specs = (
        P(("img", "txt"), None),
        P(("img", "txt"), None),
        P(),
        P(),
        P(),
        P(("img", "txt")),
        P(("img", "txt")),
    )
    out_specs = (
        P(("img", "txt"), None),
        P(("img", "txt"), None),
        P(("img", "txt"), None),
        P(("img", "txt"), None),
    )
    return jax.shard_map(shards, mesh=mesh, in_specs=in_specs, out_specs=out_specs, check_vma=False)
```

profile of v0, /device:TPU:1, one launch (start us, length us, event | category | flops | bytes accessed | tf_op | source)
XLA Modules:
  0.0 703.3 jit_solution(6278500807768814736)
XLA Ops:
  15.2 56.7 %all-gather.2.cloned.1.call-done = bf16[1024,1152]{1,0:T(8,128)(2,1)} async-done(((bf16[128,1152]{1,0:T(8,128)(2,1)}), bf16[1024,1152]{1,0:T(8,128)(2,1)}) %all-gather.2.cloned.1.call-update) | async-done | bytes 2359312 | tf_op jit(solution)/shard_map/all_gather | solution.py:55
  72.0 368.1 %while.19 = (s32[]{:T(128)}, bf16[128,1152]{1,0:T(8,128)(2,1)}, f32[128,1152]{1,0:T(8,128)S(1)}, f32[128]{0:T(128)}, f32[128]{0:T(128)}, /*index=5*/f32[1024,115...) while((s32[]{:T(128)}, bf16[128,1152]{1,0:T(8,128)(2,1)}, ...), condition=%wide.region_4.5_spmd.clone, body=%wide.region_3.4_spmd.clone.sunk | while | flops 911000576 | bytes 31341896 | solution.py:79
  103.2 5.3 fusion.66
  123.6 5.3 fusion.66
  147.4 5.3 fusion.66
  165.0 6.2 collective-permute-start.2
  171.3 5.3 fusion.66
  188.9 6.2 collective-permute-start.2
  195.1 5.3 fusion.66
  212.7 6.2 collective-permute-start.2
  218.9 5.3 fusion.66
  236.5 6.2 collective-permute-start.2
  242.8 5.3 fusion.66
  260.4 6.2 collective-permute-start.2
  266.6 5.3 fusion.66
  284.2 6.2 collective-permute-start.2
  290.5 5.3 fusion.66
  308.1 6.2 collective-permute-start.2
  314.3 5.3 fusion.66
  331.9 6.2 collective-permute-start.2
  338.2 5.3 fusion.66
  355.7 6.2 collective-permute-start.2
  362.0 5.3 fusion.66
  379.6 6.2 collective-permute-start.2
  385.8 5.3 fusion.66
  403.4 6.2 collective-permute-start.2
  409.7 5.3 fusion.66
  427.3 6.2 collective-permute-start.2
  433.5 5.3 fusion.66
  450.9 61.0 %reduce-scatter.3.cloned.1.call-done = bf16[128,1152]{1,0:T(8,128)(2,1)} async-done(((bf16[1024,1152]{1,0:T(8,128)(2,1)}), bf16[128,1152]{1,0:T(8,128)(2,1)}) %reduce-scatter.3.cloned.1.call-update) | async-done | bytes 294928 | tf_op jit(solution)/shard_map/reduce_scatter | solution.py:82
  517.4 8.8 %pad_maximum_fusion = f32[1152,2304]{0,1:T(8,128)} fusion(f32[1152,1152]{0,1:T(8,128)} %convolution_bitcast_fusion, f32[1152,1152]{0,1:T(8,128)} %convolution_bitcast_fusion.1), kind=kLoop, calls=%fused_computation.29 | loop fusion | flops 2654208 | bytes 21233664 | tf_op jit(solution)/shard_map/concatenate | solution.py:100
  531.5 159.6 %all-reduce.3.cloned.1.call-done = f32[1152,2304]{0,1:T(8,128)} async-done(((f32[1152,2304]{0,1:T(8,128)}), f32[1152,2304]{0,1:T(8,128)}) %all-reduce.3.cloned.1.call-update) | async-done | bytes 10616848
  (322 shorter events, 248.5 us)
Async XLA Ops:
  7.2 64.7 %all-gather.2.cloned.1.call-start = ((), (), s32[]{:S(2)}) async-start(), calls=%async_computation.1 | async-start | bytes 2654208 | tf_op jit(solution)/shard_map/all_gather | solution.py:55
  11.6 500.3 %reduce-scatter.3.cloned.1.call-start = ((), (), s32[]{:S(2)}) async-start(), calls=%async_computation.2 | async-start | bytes 2654208 | tf_op jit(solution)/shard_map/reduce_scatter | solution.py:82
  79.4 12.2 %collective-permute-start.1 = (f32[128,1152]{1,0:T(8,128)}, f32[128,1152]{1,0:T(8,128)S(1)}, u32[]{:S(2)}, u32[]{:S(2)}) collective-permute-start(f32[128,1152]{1,0:T(8,128)} %fusion.65), channel_id=1, source_target_pairs={{15,0},{0,1},{1,2},{2,3},{3,4},{4,5},{5,6},{6,7},{7,8},{8,9},{9,10... | collective-permute-start | bytes 1769480 | tf_op jit(solution)/shard_map/while/body/eval_jaxpr/ppermute | solution.py:13
  99.0 12.8 %collective-permute-start.1 = (f32[128,1152]{1,0:T(8,128)}, f32[128,1152]{1,0:T(8,128)S(1)}, u32[]{:S(2)}, u32[]{:S(2)}) collective-permute-start(f32[128,1152]{1,0:T(8,128)} %fusion.65), channel_id=1, source_target_pairs={{15,0},{0,1},{1,2},{2,3},{3,4},{4,5},{5,6},{6,7},{7,8},{8,9},{9,10... | collective-permute-start | bytes 1769480 | tf_op jit(solution)/shard_map/while/body/eval_jaxpr/ppermute | solution.py:13
  119.2 12.8 %collective-permute-start.1 = (f32[128,1152]{1,0:T(8,128)}, f32[128,1152]{1,0:T(8,128)S(1)}, u32[]{:S(2)}, u32[]{:S(2)}) collective-permute-start(f32[128,1152]{1,0:T(8,128)} %fusion.65), channel_id=1, source_target_pairs={{15,0},{0,1},{1,2},{2,3},{3,4},{4,5},{5,6},{6,7},{7,8},{8,9},{9,10... | collective-permute-start | bytes 1769480 | tf_op jit(solution)/shard_map/while/body/eval_jaxpr/ppermute | solution.py:13
  139.4 14.6 %collective-permute-start.1 = (f32[128,1152]{1,0:T(8,128)}, f32[128,1152]{1,0:T(8,128)S(1)}, u32[]{:S(2)}, u32[]{:S(2)}) collective-permute-start(f32[128,1152]{1,0:T(8,128)} %fusion.65), channel_id=1, source_target_pairs={{15,0},{0,1},{1,2},{2,3},{3,4},{4,5},{5,6},{6,7},{7,8},{8,9},{9,10... | collective-permute-start | bytes 1769480 | tf_op jit(solution)/shard_map/while/body/eval_jaxpr/ppermute | solution.py:13
  161.4 16.5 %collective-permute-start.1 = (f32[128,1152]{1,0:T(8,128)}, f32[128,1152]{1,0:T(8,128)S(1)}, u32[]{:S(2)}, u32[]{:S(2)}) collective-permute-start(f32[128,1152]{1,0:T(8,128)} %fusion.65), channel_id=1, source_target_pairs={{15,0},{0,1},{1,2},{2,3},{3,4},{4,5},{5,6},{6,7},{7,8},{8,9},{9,10... | collective-permute-start | bytes 1769480 | tf_op jit(solution)/shard_map/while/body/eval_jaxpr/ppermute | solution.py:13
  162.3 15.6 %collective-permute-start = (bf16[128,1152]{1,0:T(8,128)(2,1)S(1)}, bf16[128,1152]{1,0:T(8,128)(2,1)}, u32[]{:S(2)}, u32[]{:S(2)}) collective-permute-start(bf16[128,1152]{1,0:T(8,128)(2,1)S(1)} %copy.26), channel_id=1, source_target_pairs={{15,0},{0,1},{1,2},{2,3},{3,4},{4,5},{5,6},{6,7},{7,8},{8,9},{9,10... | collective-permute-start | bytes 884744 | tf_op jit(solution)/shard_map/while/body/eval_jaxpr/ppermute | solution.py:13
  185.2 16.5 %collective-permute-start.1 = (f32[128,1152]{1,0:T(8,128)}, f32[128,1152]{1,0:T(8,128)S(1)}, u32[]{:S(2)}, u32[]{:S(2)}) collective-permute-start(f32[128,1152]{1,0:T(8,128)} %fusion.65), channel_id=1, source_target_pairs={{15,0},{0,1},{1,2},{2,3},{3,4},{4,5},{5,6},{6,7},{7,8},{8,9},{9,10... | collective-permute-start | bytes 1769480 | tf_op jit(solution)/shard_map/while/body/eval_jaxpr/ppermute | solution.py:13
  185.2 16.5 %collective-permute-start = (bf16[128,1152]{1,0:T(8,128)(2,1)S(1)}, bf16[128,1152]{1,0:T(8,128)(2,1)}, u32[]{:S(2)}, u32[]{:S(2)}) collective-permute-start(bf16[128,1152]{1,0:T(8,128)(2,1)S(1)} %copy.26), channel_id=1, source_target_pairs={{15,0},{0,1},{1,2},{2,3},{3,4},{4,5},{5,6},{6,7},{7,8},{8,9},{9,10... | collective-permute-start | bytes 884744 | tf_op jit(solution)/shard_map/while/body/eval_jaxpr/ppermute | solution.py:13
  188.9 12.1 %collective-permute-start.2 = (f32[128]{0:T(128)}, f32[128]{0:T(128)}, u32[]{:S(2)}, u32[]{:S(2)}) collective-permute-start(f32[128]{0:T(128)} %copy.28), channel_id=1, source_target_pairs={{15,0},{0,1},{1,2},{2,3},{3,4},{4,5},{5,6},{6,7},{7,8},{8,9},{9,10... | collective-permute-start | bytes 1544 | tf_op jit(solution)/shard_map/while/body/eval_jaxpr/ppermute | solution.py:13
  209.1 16.5 %collective-permute-start.1 = (f32[128,1152]{1,0:T(8,128)}, f32[128,1152]{1,0:T(8,128)S(1)}, u32[]{:S(2)}, u32[]{:S(2)}) collective-permute-start(f32[128,1152]{1,0:T(8,128)} %fusion.65), channel_id=1, source_target_pairs={{15,0},{0,1},{1,2},{2,3},{3,4},{4,5},{5,6},{6,7},{7,8},{8,9},{9,10... | collective-permute-start | bytes 1769480 | tf_op jit(solution)/shard_map/while/body/eval_jaxpr/ppermute | solution.py:13
  209.1 16.5 %collective-permute-start = (bf16[128,1152]{1,0:T(8,128)(2,1)S(1)}, bf16[128,1152]{1,0:T(8,128)(2,1)}, u32[]{:S(2)}, u32[]{:S(2)}) collective-permute-start(bf16[128,1152]{1,0:T(8,128)(2,1)S(1)} %copy.26), channel_id=1, source_target_pairs={{15,0},{0,1},{1,2},{2,3},{3,4},{4,5},{5,6},{6,7},{7,8},{8,9},{9,10... | collective-permute-start | bytes 884744 | tf_op jit(solution)/shard_map/while/body/eval_jaxpr/ppermute | solution.py:13
  232.9 16.5 %collective-permute-start.1 = (f32[128,1152]{1,0:T(8,128)}, f32[128,1152]{1,0:T(8,128)S(1)}, u32[]{:S(2)}, u32[]{:S(2)}) collective-permute-start(f32[128,1152]{1,0:T(8,128)} %fusion.65), channel_id=1, source_target_pairs={{15,0},{0,1},{1,2},{2,3},{3,4},{4,5},{5,6},{6,7},{7,8},{8,9},{9,10... | collective-permute-start | bytes 1769480 | tf_op jit(solution)/shard_map/while/body/eval_jaxpr/ppermute | solution.py:13
  232.9 16.5 %collective-permute-start = (bf16[128,1152]{1,0:T(8,128)(2,1)S(1)}, bf16[128,1152]{1,0:T(8,128)(2,1)}, u32[]{:S(2)}, u32[]{:S(2)}) collective-permute-start(bf16[128,1152]{1,0:T(8,128)(2,1)S(1)} %copy.26), channel_id=1, source_target_pairs={{15,0},{0,1},{1,2},{2,3},{3,4},{4,5},{5,6},{6,7},{7,8},{8,9},{9,10... | collective-permute-start | bytes 884744 | tf_op jit(solution)/shard_map/while/body/eval_jaxpr/ppermute | solution.py:13
  256.7 16.5 %collective-permute-start.1 = (f32[128,1152]{1,0:T(8,128)}, f32[128,1152]{1,0:T(8,128)S(1)}, u32[]{:S(2)}, u32[]{:S(2)}) collective-permute-start(f32[128,1152]{1,0:T(8,128)} %fusion.65), channel_id=1, source_target_pairs={{15,0},{0,1},{1,2},{2,3},{3,4},{4,5},{5,6},{6,7},{7,8},{8,9},{9,10... | collective-permute-start | bytes 1769480 | tf_op jit(solution)/shard_map/while/body/eval_jaxpr/ppermute | solution.py:13
  256.7 16.5 %collective-permute-start = (bf16[128,1152]{1,0:T(8,128)(2,1)S(1)}, bf16[128,1152]{1,0:T(8,128)(2,1)}, u32[]{:S(2)}, u32[]{:S(2)}) collective-permute-start(bf16[128,1152]{1,0:T(8,128)(2,1)S(1)} %copy.26), channel_id=1, source_target_pairs={{15,0},{0,1},{1,2},{2,3},{3,4},{4,5},{5,6},{6,7},{7,8},{8,9},{9,10... | collective-permute-start | bytes 884744 | tf_op jit(solution)/shard_map/while/body/eval_jaxpr/ppermute | solution.py:13
  280.6 16.5 %collective-permute-start.1 = (f32[128,1152]{1,0:T(8,128)}, f32[128,1152]{1,0:T(8,128)S(1)}, u32[]{:S(2)}, u32[]{:S(2)}) collective-permute-start(f32[128,1152]{1,0:T(8,128)} %fusion.65), channel_id=1, source_target_pairs={{15,0},{0,1},{1,2},{2,3},{3,4},{4,5},{5,6},{6,7},{7,8},{8,9},{9,10... | collective-permute-start | bytes 1769480 | tf_op jit(solution)/shard_map/while/body/eval_jaxpr/ppermute | solution.py:13
  280.6 16.5 %collective-permute-start = (bf16[128,1152]{1,0:T(8,128)(2,1)S(1)}, bf16[128,1152]{1,0:T(8,128)(2,1)}, u32[]{:S(2)}, u32[]{:S(2)}) collective-permute-start(bf16[128,1152]{1,0:T(8,128)(2,1)S(1)} %copy.26), channel_id=1, source_target_pairs={{15,0},{0,1},{1,2},{2,3},{3,4},{4,5},{5,6},{6,7},{7,8},{8,9},{9,10... | collective-permute-start | bytes 884744 | tf_op jit(solution)/shard_map/while/body/eval_jaxpr/ppermute | solution.py:13
  304.4 16.5 %collective-permute-start.1 = (f32[128,1152]{1,0:T(8,128)}, f32[128,1152]{1,0:T(8,128)S(1)}, u32[]{:S(2)}, u32[]{:S(2)}) collective-permute-start(f32[128,1152]{1,0:T(8,128)} %fusion.65), channel_id=1, source_target_pairs={{15,0},{0,1},{1,2},{2,3},{3,4},{4,5},{5,6},{6,7},{7,8},{8,9},{9,10... | collective-permute-start | bytes 1769480 | tf_op jit(solution)/shard_map/while/body/eval_jaxpr/ppermute | solution.py:13
  304.4 16.5 %collective-permute-start = (bf16[128,1152]{1,0:T(8,128)(2,1)S(1)}, bf16[128,1152]{1,0:T(8,128)(2,1)}, u32[]{:S(2)}, u32[]{:S(2)}) collective-permute-start(bf16[128,1152]{1,0:T(8,128)(2,1)S(1)} %copy.26), channel_id=1, source_target_pairs={{15,0},{0,1},{1,2},{2,3},{3,4},{4,5},{5,6},{6,7},{7,8},{8,9},{9,10... | collective-permute-start | bytes 884744 | tf_op jit(solution)/shard_map/while/body/eval_jaxpr/ppermute | solution.py:13
  328.2 16.5 %collective-permute-start.1 = (f32[128,1152]{1,0:T(8,128)}, f32[128,1152]{1,0:T(8,128)S(1)}, u32[]{:S(2)}, u32[]{:S(2)}) collective-permute-start(f32[128,1152]{1,0:T(8,128)} %fusion.65), channel_id=1, source_target_pairs={{15,0},{0,1},{1,2},{2,3},{3,4},{4,5},{5,6},{6,7},{7,8},{8,9},{9,10... | collective-permute-start | bytes 1769480 | tf_op jit(solution)/shard_map/while/body/eval_jaxpr/ppermute | solution.py:13
  328.2 16.5 %collective-permute-start = (bf16[128,1152]{1,0:T(8,128)(2,1)S(1)}, bf16[128,1152]{1,0:T(8,128)(2,1)}, u32[]{:S(2)}, u32[]{:S(2)}) collective-permute-start(bf16[128,1152]{1,0:T(8,128)(2,1)S(1)} %copy.26), channel_id=1, source_target_pairs={{15,0},{0,1},{1,2},{2,3},{3,4},{4,5},{5,6},{6,7},{7,8},{8,9},{9,10... | collective-permute-start | bytes 884744 | tf_op jit(solution)/shard_map/while/body/eval_jaxpr/ppermute | solution.py:13
  352.1 16.5 %collective-permute-start.1 = (f32[128,1152]{1,0:T(8,128)}, f32[128,1152]{1,0:T(8,128)S(1)}, u32[]{:S(2)}, u32[]{:S(2)}) collective-permute-start(f32[128,1152]{1,0:T(8,128)} %fusion.65), channel_id=1, source_target_pairs={{15,0},{0,1},{1,2},{2,3},{3,4},{4,5},{5,6},{6,7},{7,8},{8,9},{9,10... | collective-permute-start | bytes 1769480 | tf_op jit(solution)/shard_map/while/body/eval_jaxpr/ppermute | solution.py:13
  352.1 16.5 %collective-permute-start = (bf16[128,1152]{1,0:T(8,128)(2,1)S(1)}, bf16[128,1152]{1,0:T(8,128)(2,1)}, u32[]{:S(2)}, u32[]{:S(2)}) collective-permute-start(bf16[128,1152]{1,0:T(8,128)(2,1)S(1)} %copy.26), channel_id=1, source_target_pairs={{15,0},{0,1},{1,2},{2,3},{3,4},{4,5},{5,6},{6,7},{7,8},{8,9},{9,10... | collective-permute-start | bytes 884744 | tf_op jit(solution)/shard_map/while/body/eval_jaxpr/ppermute | solution.py:13
  375.9 16.5 %collective-permute-start.1 = (f32[128,1152]{1,0:T(8,128)}, f32[128,1152]{1,0:T(8,128)S(1)}, u32[]{:S(2)}, u32[]{:S(2)}) collective-permute-start(f32[128,1152]{1,0:T(8,128)} %fusion.65), channel_id=1, source_target_pairs={{15,0},{0,1},{1,2},{2,3},{3,4},{4,5},{5,6},{6,7},{7,8},{8,9},{9,10... | collective-permute-start | bytes 1769480 | tf_op jit(solution)/shard_map/while/body/eval_jaxpr/ppermute | solution.py:13
  375.9 16.5 %collective-permute-start = (bf16[128,1152]{1,0:T(8,128)(2,1)S(1)}, bf16[128,1152]{1,0:T(8,128)(2,1)}, u32[]{:S(2)}, u32[]{:S(2)}) collective-permute-start(bf16[128,1152]{1,0:T(8,128)(2,1)S(1)} %copy.26), channel_id=1, source_target_pairs={{15,0},{0,1},{1,2},{2,3},{3,4},{4,5},{5,6},{6,7},{7,8},{8,9},{9,10... | collective-permute-start | bytes 884744 | tf_op jit(solution)/shard_map/while/body/eval_jaxpr/ppermute | solution.py:13
  399.8 16.5 %collective-permute-start.1 = (f32[128,1152]{1,0:T(8,128)}, f32[128,1152]{1,0:T(8,128)S(1)}, u32[]{:S(2)}, u32[]{:S(2)}) collective-permute-start(f32[128,1152]{1,0:T(8,128)} %fusion.65), channel_id=1, source_target_pairs={{15,0},{0,1},{1,2},{2,3},{3,4},{4,5},{5,6},{6,7},{7,8},{8,9},{9,10... | collective-permute-start | bytes 1769480 | tf_op jit(solution)/shard_map/while/body/eval_jaxpr/ppermute | solution.py:13
  399.8 16.5 %collective-permute-start = (bf16[128,1152]{1,0:T(8,128)(2,1)S(1)}, bf16[128,1152]{1,0:T(8,128)(2,1)}, u32[]{:S(2)}, u32[]{:S(2)}) collective-permute-start(bf16[128,1152]{1,0:T(8,128)(2,1)S(1)} %copy.26), channel_id=1, source_target_pairs={{15,0},{0,1},{1,2},{2,3},{3,4},{4,5},{5,6},{6,7},{7,8},{8,9},{9,10... | collective-permute-start | bytes 884744 | tf_op jit(solution)/shard_map/while/body/eval_jaxpr/ppermute | solution.py:13
  423.6 16.5 %collective-permute-start.1 = (f32[128,1152]{1,0:T(8,128)}, f32[128,1152]{1,0:T(8,128)S(1)}, u32[]{:S(2)}, u32[]{:S(2)}) collective-permute-start(f32[128,1152]{1,0:T(8,128)} %fusion.65), channel_id=1, source_target_pairs={{15,0},{0,1},{1,2},{2,3},{3,4},{4,5},{5,6},{6,7},{7,8},{8,9},{9,10... | collective-permute-start | bytes 1769480 | tf_op jit(solution)/shard_map/while/body/eval_jaxpr/ppermute | solution.py:13
  423.6 16.5 %collective-permute-start = (bf16[128,1152]{1,0:T(8,128)(2,1)S(1)}, bf16[128,1152]{1,0:T(8,128)(2,1)}, u32[]{:S(2)}, u32[]{:S(2)}) collective-permute-start(bf16[128,1152]{1,0:T(8,128)(2,1)S(1)} %copy.26), channel_id=1, source_target_pairs={{15,0},{0,1},{1,2},{2,3},{3,4},{4,5},{5,6},{6,7},{7,8},{8,9},{9,10... | collective-permute-start | bytes 884744 | tf_op jit(solution)/shard_map/while/body/eval_jaxpr/ppermute | solution.py:13
  444.1 247.0 %all-reduce.3.cloned.1.call-start = ((), (), s32[]{:S(2)}) async-start(), calls=%async_computation.3 | async-start | bytes 21233664
  (75 other events, 540.5 us)
Sparse Core Ops, SparseCore 0:
  11.8 60.1 all-gather.1
  444.2 67.6 reduce-scatter.2
  526.3 164.7 all-reduce.2
where the time goes:
time: 705 us; the launch traced here: 703 us
  waiting for transfers between devices  305 us (43%)
  matrix products  163 us (23%)
  starting transfers between devices  139 us (20%)
  local copies, waits for them, and re-layouts  62.8 us (9%)
  other arithmetic  19.3 us (3%)
  between operations  13.9 us (2%)
    unnamed x4, waiting for transfers between devices  160 us
    ppermute x64, starting transfers between devices, passed_along(): return lax.ppermute(block, axis, route)  139 us
    dot_general x16, matrix products, pair_tile(): jnp.dot(slopes, panel_rows, preferred_element_type=jnp.float32)  83.6 us
    reduce_scatter x1, waiting for transfers between devices, shards(): lax.psum_scatter(image_acc.astype(jnp.bfloat16), 'img', scatter_dimension...  61 us
    all_gather x1, waiting for transfers between devices, shards(): images = lax.all_gather(unit_img, 'img', axis=0, tiled=True)  56.7 us
    while x112, local copies, waits for them, and re-layouts  55.5 us
    dot_general x16, matrix products, pair_tile(): lax.dot_general(images, panel_rows, (((1,), (1,)), ((), ())), preferred_e...  40.1 us
    ppermute x64, waiting for transfers between devices, passed_along(): return lax.ppermute(block, axis, route)  27.4 us
  transfers between devices with their start and end apart: 67, of which 32 were waited for; matrix products, arithmetic and copies ran while one was open for 14% of the time, Pallas kernels for 0%

commit v1 on v0

v1 whole, which is shorter than its diff:
```python
import jax
import jax.numpy as jnp
from jax import lax
from jax.sharding import PartitionSpec as P

logit_scale = 64.0
epsilon = 1e-06

PLACE = ("z", "lo", "hi", "y", "core")
IMG = ("z", "lo")
TXT = ("hi", "y")


def exchange(blocks, axes):
    return lax.all_to_all(blocks, axes, 0, 0, tiled=True)


def gather(own, axes):
    blocks = jnp.broadcast_to(own[None], (8,) + own.shape)
    return exchange(blocks, axes).reshape((8 * own.shape[0],) + own.shape[1:])


def core_swap(block):
    return lax.ppermute(block, "core", [(0, 1), (1, 0)])


def unit_columns(feats, head):
    projected = lax.dot_general(
        head, feats, (((0,), (1,)), ((), ())), preferred_element_type=jnp.float32
    )
    norm = jnp.sqrt(jnp.sum(projected * projected, axis=0, keepdims=True) + epsilon)
    return projected, norm, (projected / norm).astype(jnp.bfloat16)


def pair_tile(unit_img, unit_txt, image_ids, bias, partner):
    cosines = logit_scale * lax.dot_general(
        unit_img, unit_txt, (((0,), (0,)), ((), ())), preferred_element_type=jnp.float32
    )
    positive = (partner[None, :] == image_ids[:, None]).astype(jnp.float32)
    slopes = (jax.nn.sigmoid(cosines + bias[None, :]) - positive).astype(jnp.bfloat16)
    weighted = slopes.astype(jnp.float32) * cosines
    return slopes, jnp.sum(weighted, axis=1), jnp.sum(weighted, axis=0)


def shards(image_feat, text_feat, image_head, text_head, group_bias, text_lang, partner):
    f32, b16 = jnp.float32, jnp.bfloat16
    rows, width = image_feat.shape
    slab = width // 8
    out_rows = width // 128
    core = lax.axis_index("core")
    img_place = lax.axis_index(IMG)
    txt_place = lax.axis_index(TXT)

    is_group = text_lang[:, None] == jnp.arange(group_bias.shape[0], dtype=jnp.int32)[None, :]
    text_bias = jnp.sum(jnp.where(is_group, group_bias[None, :], 0.0), axis=1)
    meta = jnp.stack([text_bias, partner.astype(f32)])
    meta = lax.all_gather(meta, TXT + ("core",), axis=0, tiled=False)
    meta = meta.reshape(8, 2, 2, rows).transpose(1, 2, 0, 3).reshape(2, 2, 8 * rows)

    txt_feats = gather(text_feat, TXT)
    img_feats = gather(image_feat, IMG)

    index = jnp.arange(8 * rows, dtype=jnp.int32)
    image_ids = index // rows * 16 + txt_place * 2 + core
    image_ids = (image_ids * rows + index % rows).astype(f32)

    proj_txt, norm_txt, unit_txt = unit_columns(txt_feats, text_head)
    other_txt = core_swap(unit_txt)
    proj_img, norm_img, unit_img = unit_columns(img_feats, image_head)

    mine = lax.dynamic_index_in_dim(meta, core, 0, keepdims=False)
    theirs = lax.dynamic_index_in_dim(meta, 1 - core, 0, keepdims=False)
    slopes, img_sum, txt_sum = pair_tile(unit_img, unit_txt, image_ids, mine[0], mine[1])
    other_slopes, other_img_sum, other_txt_sum = pair_tile(
        unit_img, other_txt, image_ids, theirs[0], theirs[1]
    )
    other_up = lax.dot_general(
        unit_img, other_slopes, (((1,), (0,)), ((), ())), preferred_element_type=f32
    ).astype(b16)
    back_up = core_swap(other_up)

    img_sum = lax.psum(img_sum + other_img_sum, IMG)
    txt_sum = lax.psum(txt_sum + core_swap(other_txt_sum), TXT)

    image_up = lax.dot_general(
        unit_txt, slopes, (((1,), (1,)), ((), ())), preferred_element_type=f32
    ) + lax.dot_general(
        other_txt, other_slopes, (((1,), (1,)), ((), ())), preferred_element_type=f32
    )
    image_up = exchange(image_up.astype(b16).reshape(8, slab, 8 * rows), IMG)
    text_up = lax.dot_general(
        unit_img, slopes, (((1,), (0,)), ((), ())), preferred_element_type=f32
    ) + back_up.astype(f32)
    text_up = exchange(text_up.astype(b16).reshape(8, slab, 8 * rows), TXT)

    def back_norm(projected, norm, upstream, inner, place):
        upstream = logit_scale * jnp.sum(upstream.astype(f32), axis=0)
        projected = lax.dynamic_slice_in_dim(projected, place * slab, slab, axis=0)
        return ((upstream - projected * (inner[None, :] / norm)) / norm).astype(b16)

    grad_img = back_norm(proj_img, norm_img, image_up, img_sum, img_place)
    grad_txt = back_norm(proj_txt, norm_txt, text_up, txt_sum, txt_place)

    def feature_grad(grad, head, axes):
        blocks = grad.reshape(slab, 8, rows).transpose(1, 0, 2)
        whole = exchange(blocks, axes).reshape(width, rows)
        return lax.dot_general(whole, head, (((0,), (1,)), ((), ())), preferred_element_type=f32)

    image_grad = feature_grad(grad_img, image_head, IMG)
    text_grad = feature_grad(grad_txt, text_head, TXT)

    def head_part(feats, grad):
        return lax.dot_general(feats, grad, (((0,), (1,)), ((), ())), preferred_element_type=f32)

    part = jnp.concatenate([head_part(img_feats, grad_img), head_part(txt_feats, grad_txt)], axis=1)
    part = exchange(part.astype(b16).reshape(128, out_rows, 2 * slab), PLACE).astype(f32)
    part = part.reshape(8, 8, 2, out_rows, 2 * slab)
    image_head_grad = jnp.sum(part[..., :slab], axis=(1, 2))
    text_head_grad = jnp.sum(part[..., slab:], axis=(0, 2))
    image_head_grad = image_head_grad.transpose(1, 0, 2).reshape(out_rows, width)
    text_head_grad = text_head_grad.transpose(1, 0, 2).reshape(out_rows, width)
    return (image_grad, text_grad, image_head_grad, text_head_grad)


def solution(mesh):
    places = jax.sharding.Mesh(mesh.devices.reshape(4, 2, 2, 4, 2), PLACE)
    rows = P(PLACE, None)
    row = P(PLACE)
    in_specs = (rows, rows, P(), P(), P(), row, row)
    return jax.shard_map(
        shards, mesh=places, in_specs=in_specs, out_specs=(rows,) * 4, check_vma=False
    )
```

time: 705 us -> 309 us (0.44)
  waiting for transfers between devices: 305 us -> 56.6 us
  matrix products: 163 us -> 55.9 us
  blocking collectives: 0 us -> 99.8 us
  starting transfers between devices: 139 us -> 48.2 us
  local copies, waits for them, and re-layouts: 62.8 us -> 28.9 us
  between operations: 13.9 us -> 0.94 us
    unnamed x4 -> x0, waiting for transfers between devices: 160 us -> none
    ppermute x64 -> x3, starting transfers between devices: 139 us -> 2.7 us  [core_swap(): return lax.ppermute(block, 'core', [(0, 1), (1, 0)])]
    dot_general x54 -> x12, matrix products: 163 us -> 55.9 us  [the longest x2 13.7 us: pair_tile(): lax.dot_general(unit_img, unit_txt, (((0,), (0,)), ((), ())), preferred_e...]
    reduce_scatter x1 -> x0, waiting for transfers between devices: 61 us -> none  [shards(): lax.psum_scatter(image_acc.astype(jnp.bfloat16), 'img', scatter_dimension...]
    all_gather x1 -> x0, waiting for transfers between devices: 56.7 us -> none  [shards(): images = lax.all_gather(unit_img, 'img', axis=0, tiled=True)]
    all_to_all x0 -> x7, waiting for transfers between devices: none -> 56.6 us  [exchange(): return lax.all_to_all(blocks, axes, 0, 0, tiled=True)]
    psum x0 -> x2, blocking collectives: none -> 55.8 us  [the longest x1 34.7 us: shards(): img_sum = lax.psum(img_sum + other_img_sum, IMG)]
    while x112 -> x0, local copies, waits for them, and re-layouts: 55.5 us -> none
  transfers between devices with their start and end apart: 67 -> 10, of which waited for: 32 -> 4; matrix products, arithmetic and copies ran while one was open for 14% -> 22% of each run, Pallas kernels for 0% -> 0%
where the time goes in v1:
time: 309 us; the launch traced here: 307 us
  blocking collectives  99.8 us (32%)
  waiting for transfers between devices  56.6 us (18%)
  matrix products  55.9 us (18%)
  starting transfers between devices  48.2 us (16%)
  local copies, waits for them, and re-layouts  28.9 us (9%)
  other arithmetic  17 us (6%)
    all_to_all x7, waiting for transfers between devices, exchange(): return lax.all_to_all(blocks, axes, 0, 0, tiled=True)  56.6 us
    all_to_all x7, starting transfers between devices, exchange(): return lax.all_to_all(blocks, axes, 0, 0, tiled=True)  45.5 us
    all_gather x1, blocking collectives, shards(): meta = lax.all_gather(meta, TXT + ('core',), axis=0, tiled=False)  44 us
    psum x1, blocking collectives, shards(): img_sum = lax.psum(img_sum + other_img_sum, IMG)  34.7 us
    psum x1, blocking collectives, shards(): txt_sum = lax.psum(txt_sum + core_swap(other_txt_sum), TXT)  21.1 us
    dot_general x2, matrix products, pair_tile(): lax.dot_general(unit_img, unit_txt, (((0,), (0,)), ((), ())), preferred_e...  13.7 us
    dot_general x2, matrix products, unit_columns(): lax.dot_general(head, feats, (((0,), (1,)), ((), ())), preferred_element_...  10.7 us
    unnamed x28, local copies, waits for them, and re-layouts  9.27 us
  transfers between devices with their start and end apart: 10, of which 4 were waited for; matrix products, arithmetic and copies ran while one was open for 22% of the time, Pallas kernels for 0%

profile of v1, /device:TPU:1, one launch (start us, length us, event | category | flops | bytes accessed | tf_op | source)
XLA Modules:
  0.0 307.3 jit_solution(156395569584746917)
XLA Ops:
  0.6 2.8 broadcast_in_dim.16
  3.5 7.6 %all-to-all-start = ((bf16[8,128,1152]{2,1,0:T(8,128)(2,1)}), bf16[8,128,1152]{2,1,0:T(8,128)(2,1)}, u32[]{:S(2)}, u32[]{:S(2)}) async-start(bf16[8,128,1152]{2,1,0:T(8,128)(2,1)} %broadcast_in_dim.16), calls=%async_computation | async-start | bytes 4718592 | tf_op jit(solution)/shard_map/all_to_all | solution.py:15
  11.2 44.0 %all-gather.1 = f32[16,2,128]{2,1,0:T(2,128)S(1)} all-gather(f32[1,2,128]{2,1,0:T(2,128)S(1)} %maximum_bitcast_fusion), channel_id=2, replica_groups=mesh['z'=4,'lo'=2,'hi'=2,'y'=4,'core'=2] {'hi','y','core'}, dimensions={0}, use_global_device_ids=true | all-gather | bytes 17408 | tf_op jit(solution)/shard_map/all_gather | solution.py:57
  57.0 5.1 %all-to-all-start.1 = ((bf16[8,128,1152]{2,1,0:T(8,128)(2,1)}), bf16[8,128,1152]{2,1,0:T(8,128)(2,1)}, u32[]{:S(2)}, u32[]{:S(2)}) async-start(bf16[8,128,1152]{2,1,0:T(8,128)(2,1)} %broadcast_in_dim.17), calls=%async_computation.1 | async-start | bytes 4718592 | tf_op jit(solution)/shard_map/all_to_all | solution.py:15
  62.1 5.8 %multiply_reduce_fusion.1 = (f32[1024]{0:T(1024)S(1)}, f32[1152,1024]{1,0:T(8,128)S(1)}) fusion(bf16[1152,1152]{1,0:T(8,128)(2,1)} %param.10, bf16[1024,1152]{1,0:T(8,128)(2,1)} %bitcast), kind=kOutput, calls=%fused_computation.7 | convolution fusion | flops 2720267264 | bytes 9736192 | tf_op jit(solution)/shard_map/dot_general | solution.py:28
  67.9 2.5 divide_convert_fusion.1
  71.2 20.4 %all-to-all-done.1 = bf16[8,128,1152]{2,1,0:T(8,128)(2,1)} async-done(((bf16[8,128,1152]{2,1,0:T(8,128)(2,1)}), bf16[8,128,1152]{2,1,0:T(8,128)(2,1)}, u32[]{:S(2)}, u32[]{:S(2)}) %all-to-all-start.1) | async-done | bytes 2359328 | tf_op jit(solution)/shard_map/all_to_all | solution.py:15
  91.6 5.0 %multiply_reduce_fusion = (f32[1024]{0:T(1024)S(1)}, f32[1152,1024]{1,0:T(8,128)S(1)}) fusion(bf16[1152,1152]{1,0:T(8,128)(2,1)S(1)} %copy-done, bf16[1024,1152]{1,0:T(8,128)(2,1)} %bitcast.1), kind=kOutput, calls=%fused_computation.5 | convolution fusion | flops 2720267264 | bytes 9736192 | tf_op jit(solution)/shard_map/dot_general | solution.py:28
  98.7 5.4 %fusion.19 = f32[1024,1024]{1,0:T(8,128)S(1)} fusion(bf16[1152,1024]{1,0:T(8,128)(2,1)S(1)} %divide_convert_fusion, bf16[1152,1024]{1,0:T(8,128)(2,1)} %divide_convert_fusion.1), kind=kOutput, calls=%fused_computation.58 | convolution fusion | flops 2415919104 | bytes 8912896 | tf_op jit(solution)/shard_map/dot_general | solution.py:36
  104.2 8.3 %fusion.2 = (f32[1024]{0:T(1024)S(1)}, f32[1024]{0:T(1024)S(1)}, bf16[1024,1024]{1,0:T(8,128)(2,1)S(1)}, f32[1024]{0:T(1024)S(1)}, f32[1024]{0:T(1024)S(1)}, /*index=5*/bf16[1024,1024]{1,0:T(8,128)(2,1)S(1)}) fusion(f32[1024]{0:T(1024)S(1)} %fusion.17, f32[1024]{0:T(1024)S(1)} %bitcast.79, f32[1024]{0:T(1024)S(1)} %bitcast.77, f32[1024]{0:T(1024)S(1)} %bitcast.80, ...), kind=kOutput, calls=%fused_computation.15 | convolution fusion | flops 2443177984 | bytes 13144064 | tf_op jit(solution)/shard_map/dot_general | solution.py:36
  112.5 3.8 %convolution_convert_fusion = bf16[1152,1024]{1,0:T(8,128)(2,1)} fusion(bf16[1152,1024]{1,0:T(8,128)(2,1)S(1)} %divide_convert_fusion, bf16[1024,1024]{1,0:T(8,128)(2,1)S(1)} %get-tuple-element.10), kind=kOutput, calls=%fused_computation.12 | convolution fusion | flops 2417098752 | bytes 6815744 | tf_op jit(solution)/shard_map/dot_general | solution.py:77
  117.6 4.3 %fusion.20 = f32[1152,1024]{1,0:T(8,128)S(1)} fusion(bf16[1152,1024]{1,0:T(8,128)(2,1)} %divide_convert_fusion.1, bf16[1024,1024]{1,0:T(8,128)(2,1)S(1)} %get-tuple-element.18), kind=kOutput, calls=%fused_computation.59 | convolution fusion | flops 2415919104 | bytes 9175040 | tf_op jit(solution)/shard_map/dot_general | solution.py:85
  122.0 5.7 %add_convert_fusion.1 = bf16[1152,1024]{1,0:T(8,128)(2,1)} fusion(f32[1152,1024]{1,0:T(8,128)S(1)} %fusion.20, bf16[1152,1024]{1,0:T(8,128)(2,1)} %collective-permute-done, bf16[1024,1024]{1,0:T(8,128)(2,1)S(1)} %get-tuple-element.10), kind=kOutput, calls=%fused_computation.3 | convolution fusion | flops 2418278400 | bytes 11534336 | tf_op jit(solution)/shard_map/dot_general | solution.py:87
  127.7 4.4 %all-to-all-start.2 = ((bf16[8,144,1024]{2,1,0:T(8,128)(2,1)}), bf16[8,144,1024]{2,1,0:T(8,128)(2,1)}, u32[]{:S(2)}, u32[]{:S(2)}) async-start(bf16[8,144,1024]{2,1,0:T(8,128)(2,1)} %bitcast.70), calls=%async_computation.2 | async-start | bytes 4718592 | tf_op jit(solution)/shard_map/all_to_all | solution.py:15
  132.1 7.1 %add_convert_fusion = bf16[1152,1024]{1,0:T(8,128)(2,1)} fusion(bf16[1152,1024]{1,0:T(8,128)(2,1)} %collective-permute-done.1, bf16[1152,1024]{1,0:T(8,128)(2,1)} %copy-done.4, bf16[1024,1024]{1,0:T(8,128)(2,1)} %copy-done.12), kind=kOutput, calls=%fused_computation.1 | convolution fusion | flops 2419458048 | bytes 9175040 | tf_op jit(solution)/shard_map/dot_general | solution.py:91
  139.1 22.9 %all-to-all-done.2 = bf16[8,144,1024]{2,1,0:T(8,128)(2,1)} async-done(((bf16[8,144,1024]{2,1,0:T(8,128)(2,1)}), bf16[8,144,1024]{2,1,0:T(8,128)(2,1)}, u32[]{:S(2)}, u32[]{:S(2)}) %all-to-all-start.2) | async-done | bytes 2359328 | tf_op jit(solution)/shard_map/all_to_all | solution.py:15
  162.1 4.4 %all-to-all-start.4 = ((bf16[8,144,1024]{2,1,0:T(8,128)(2,1)}), bf16[8,144,1024]{2,1,0:T(8,128)(2,1)}, u32[]{:S(2)}, u32[]{:S(2)}) async-start(bf16[8,144,1024]{2,1,0:T(8,128)(2,1)} %bitcast.69), calls=%async_computation.4 | async-start | bytes 4718592 | tf_op jit(solution)/shard_map/all_to_all | solution.py:15
  167.4 34.7 %psum.14 = f32[1024]{0:T(1024)S(1)} all-reduce(f32[1024]{0:T(1024)S(1)} %add.142), channel_id=1, replica_groups=mesh['z'=4,'lo'=2,'hi'=2,'y'=4,'core'=2] {'z','lo'}, use_global_device_ids=true, to_apply=%region_6.7 | all-reduce | flops 1024 | bytes 8192 | tf_op jit(solution)/shard_map/psum | solution.py:82
  202.1 21.1 %psum.15 = f32[1024]{0:T(1024)S(1)} all-reduce(f32[1024]{0:T(1024)S(1)} %add.145), channel_id=1, replica_groups=mesh['z'=4,'lo'=2,'hi'=2,'y'=4,'core'=2] {'hi','y'}, use_global_device_ids=true, to_apply=%region_10.11 | all-reduce | flops 1024 | bytes 8192 | tf_op jit(solution)/shard_map/psum | solution.py:83
  226.6 3.0 fusion.4
  232.8 3.4 %all-to-all-start.3 = ((bf16[8,144,128]{2,1,0:T(8,128)(2,1)}), bf16[8,144,128]{2,1,0:T(8,128)(2,1)S(1)}, u32[]{:S(2)}, u32[]{:S(2)}) async-start(bf16[8,144,128]{2,1,0:T(8,128)(2,1)} %bitcast_bitcast_fusion.1), calls=%async_computation.3 | async-start | bytes 589824 | tf_op jit(solution)/shard_map/all_to_all | solution.py:15
  242.5 3.4 %all-to-all-start.5 = ((bf16[8,144,128]{2,1,0:T(8,128)(2,1)}), bf16[8,144,128]{2,1,0:T(8,128)(2,1)S(1)}, u32[]{:S(2)}, u32[]{:S(2)}) async-start(bf16[8,144,128]{2,1,0:T(8,128)(2,1)} %bitcast_bitcast_fusion), calls=%async_computation.5 | async-start | bytes 589824 | tf_op jit(solution)/shard_map/all_to_all | solution.py:15
  245.9 3.0 fusion.5
  251.3 3.3 %pad_maximum_fusion = bf16[128,9,288]{2,1,0:T(8,128)(2,1)} fusion(bf16[128,9,144]{2,1,0:T(8,128)(2,1)} %concatenate.10, bf16[128,9,144]{2,1,0:T(8,128)(2,1)} %concatenate.9), kind=kLoop, calls=%fused_computation.21 | loop fusion | flops 1327104 | bytes 1327104 | tf_op jit(solution)/shard_map/concatenate | solution.py:115
  254.7 4.1 %reshape.132 = bf16[128,2,1296]{2,1,0:T(2,128)(2,1)} reshape(bf16[128,9,288]{2,1,0:T(8,128)(2,1)} %pad_maximum_fusion) | data formatting | bytes 1327104
  259.4 17.2 %all-to-all-start.6 = ((bf16[128,2,1296]{2,1,0:T(2,128)(2,1)}), bf16[128,2,1296]{2,1,0:T(2,128)(2,1)S(1)}, u32[]{:S(2)}, u32[]{:S(2)}) async-start(bf16[128,2,1296]{2,1,0:T(2,128)(2,1)} %reshape.132), calls=%async_computation.6 | async-start | bytes 1441792 | tf_op jit(solution)/shard_map/all_to_all | solution.py:15
  276.7 2.9 fusion.21
  281.3 11.2 %all-to-all-done.6 = bf16[128,2,1296]{2,1,0:T(2,128)(2,1)S(1)} async-done(((bf16[128,2,1296]{2,1,0:T(2,128)(2,1)}), bf16[128,2,1296]{2,1,0:T(2,128)(2,1)S(1)}, u32[]{:S(2)}, u32[]{:S(2)}) %all-to-all-start.6) | async-done | bytes 663584 | tf_op jit(solution)/shard_map/all_to_all | solution.py:15
  292.5 2.7 reshape.133
  295.2 2.4 copy.65
  299.1 3.2 %reshape.124 = f32[8,8,2,9,288]{4,2,1,0,3:T(2,128)} reshape(f32[128,9,288]{2,0,1:T(8,128)} %copy.66) | data formatting | bytes 2654208 | tf_op jit(solution)/shard_map/reshape | solution.py:117
  302.3 3.5 %slice_reduce_fusion = (f32[8,9,144]{2,0,1:T(8,128)S(1)}, f32[8,9,144]{2,0,1:T(8,128)S(1)}) fusion(f32[8,8,2,9,288]{4,2,1,0,3:T(2,128)} %reshape.124), kind=kLoop, calls=%fused_computation.22 | loop fusion | flops 311040 | bytes 1410048 | tf_op jit(solution)/shard_map/reduce_sum | solution.py:119
  (65 shorter events, 27.8 us)
Async XLA Ops:
  0.6 90.9 %copy-start = (bf16[1152,1152]{1,0:T(8,128)(2,1)S(1)}, bf16[1152,1152]{1,0:T(8,128)(2,1)}, u32[]{:S(2)}) copy-start(bf16[1152,1152]{1,0:T(8,128)(2,1)} %param.9) | copy-start | bytes 7962628
  3.5 7.6 %copy-start.9 = (f32[32]{0:T(128)S(1)}, f32[32]{0:T(128)}, u32[]{:S(2)}) copy-start(f32[32]{0:T(128)} %param.11) | copy-start | bytes 388
  3.5 7.6 %copy-start.10 = (s32[128]{0:T(128)S(1)}, s32[128]{0:T(128)}, u32[]{:S(2)}) copy-start(s32[128]{0:T(128)} %param.12) | copy-start | bytes 1540
  3.5 7.7 %copy-start.11 = (s32[128]{0:T(128)S(1)}, s32[128]{0:T(128)}, u32[]{:S(2)}) copy-start(s32[128]{0:T(128)} %param.13) | copy-start | bytes 1540
  3.5 51.8 %copy-start.8 = (bf16[128,1152]{1,0:T(8,128)(2,1)S(1)}, bf16[128,1152]{1,0:T(8,128)(2,1)}, u32[]{:S(2)}) copy-start(bf16[128,1152]{1,0:T(8,128)(2,1)} %param.7) | copy-start | bytes 884740
  3.5 51.8 %all-to-all-start = ((bf16[8,128,1152]{2,1,0:T(8,128)(2,1)}), bf16[8,128,1152]{2,1,0:T(8,128)(2,1)}, u32[]{:S(2)}, u32[]{:S(2)}) async-start(bf16[8,128,1152]{2,1,0:T(8,128)(2,1)} %broadcast_in_dim.16), calls=%async_computation | async-start | bytes 4718592 | tf_op jit(solution)/shard_map/all_to_all | solution.py:15
  57.0 34.6 %all-to-all-start.1 = ((bf16[8,128,1152]{2,1,0:T(8,128)(2,1)}), bf16[8,128,1152]{2,1,0:T(8,128)(2,1)}, u32[]{:S(2)}, u32[]{:S(2)}) async-start(bf16[8,128,1152]{2,1,0:T(8,128)(2,1)} %broadcast_in_dim.17), calls=%async_computation.1 | async-start | bytes 4718592 | tf_op jit(solution)/shard_map/all_to_all | solution.py:15
  67.8 2.9 copy-start.1
  70.7 33.4 %collective-permute-start = (bf16[1152,1024]{1,0:T(8,128)(2,1)}, bf16[1152,1024]{1,0:T(8,128)(2,1)}, u32[]{:S(2)}, u32[]{:S(2)}) collective-permute-start(bf16[1152,1024]{1,0:T(8,128)(2,1)} %divide_convert_fusion.1), channel_id=1, source_target_pairs={{0,1},{1,0},{2,3},{3,2},{4,5},{5,4},{6,7},{7,6},{8,9},{9,8},{10,11... | collective-permute-start | bytes 7077896 | tf_op jit(solution)/shard_map/ppermute | solution.py:24
  96.5 2.2 copy-start.2
  98.7 13.8 %copy-start.4 = (bf16[1152,1024]{1,0:T(8,128)(2,1)}, bf16[1152,1024]{1,0:T(8,128)(2,1)S(1)}, u32[]{:S(2)}) copy-start(bf16[1152,1024]{1,0:T(8,128)(2,1)S(1)} %divide_convert_fusion) | copy-start | bytes 7077892
  112.5 5.2 %copy-start.12 = (bf16[1024,1024]{1,0:T(8,128)(2,1)}, bf16[1024,1024]{1,0:T(8,128)(2,1)S(1)}, u32[]{:S(2)}) copy-start(bf16[1024,1024]{1,0:T(8,128)(2,1)S(1)} %get-tuple-element.18) | copy-start | bytes 6291460
  116.3 15.8 %collective-permute-start.1 = (bf16[1152,1024]{1,0:T(8,128)(2,1)}, bf16[1152,1024]{1,0:T(8,128)(2,1)}, u32[]{:S(2)}, u32[]{:S(2)}) collective-permute-start(bf16[1152,1024]{1,0:T(8,128)(2,1)} %convolution_convert_fusion), channel_id=1, source_target_pairs={{0,1},{1,0},{2,3},{3,2},{4,5},{5,4},{6,7},{7,6},{8,9},{9,8},{10,11... | collective-permute-start | bytes 7077896 | tf_op jit(solution)/shard_map/ppermute | solution.py:24
  127.7 34.3 %all-to-all-start.2 = ((bf16[8,144,1024]{2,1,0:T(8,128)(2,1)}), bf16[8,144,1024]{2,1,0:T(8,128)(2,1)}, u32[]{:S(2)}, u32[]{:S(2)}) async-start(bf16[8,144,1024]{2,1,0:T(8,128)(2,1)} %bitcast.70), calls=%async_computation.2 | async-start | bytes 4718592 | tf_op jit(solution)/shard_map/all_to_all | solution.py:15
  162.1 70.8 %all-to-all-start.4 = ((bf16[8,144,1024]{2,1,0:T(8,128)(2,1)}), bf16[8,144,1024]{2,1,0:T(8,128)(2,1)}, u32[]{:S(2)}, u32[]{:S(2)}) async-start(bf16[8,144,1024]{2,1,0:T(8,128)(2,1)} %bitcast.69), calls=%async_computation.4 | async-start | bytes 4718592 | tf_op jit(solution)/shard_map/all_to_all | solution.py:15
  166.4 35.7 %collective-permute-start.2 = (f32[1024]{0:T(1024)S(1)}, f32[1024]{0:T(1024)S(1)}, u32[]{:S(2)}, u32[]{:S(2)}) collective-permute-start(f32[1024]{0:T(1024)S(1)} %get-tuple-element.4), channel_id=1, source_target_pairs={{0,1},{1,0},{2,3},{3,2},{4,5},{5,4},{6,7},{7,6},{8,9},{9,8},{10,11... | collective-permute-start | bytes 12296 | tf_op jit(solution)/shard_map/ppermute | solution.py:24
  232.8 9.7 %all-to-all-start.3 = ((bf16[8,144,128]{2,1,0:T(8,128)(2,1)}), bf16[8,144,128]{2,1,0:T(8,128)(2,1)S(1)}, u32[]{:S(2)}, u32[]{:S(2)}) async-start(bf16[8,144,128]{2,1,0:T(8,128)(2,1)} %bitcast_bitcast_fusion.1), calls=%async_computation.3 | async-start | bytes 589824 | tf_op jit(solution)/shard_map/all_to_all | solution.py:15
  242.5 3.4 %copy-start.5 = (bf16[8,144,128]{2,1,0:T(8,128)(2,1)}, bf16[8,144,128]{2,1,0:T(8,128)(2,1)S(1)}, u32[]{:S(2)}) copy-start(bf16[8,144,128]{2,1,0:T(8,128)(2,1)S(1)} %all-to-all-done.3) | copy-start | bytes 884740
  242.5 16.2 %all-to-all-start.5 = ((bf16[8,144,128]{2,1,0:T(8,128)(2,1)}), bf16[8,144,128]{2,1,0:T(8,128)(2,1)S(1)}, u32[]{:S(2)}, u32[]{:S(2)}) async-start(bf16[8,144,128]{2,1,0:T(8,128)(2,1)} %bitcast_bitcast_fusion), calls=%async_computation.5 | async-start | bytes 589824 | tf_op jit(solution)/shard_map/all_to_all | solution.py:15
  258.7 0.7 copy-start.6
  259.4 33.0 %all-to-all-start.6 = ((bf16[128,2,1296]{2,1,0:T(2,128)(2,1)}), bf16[128,2,1296]{2,1,0:T(2,128)(2,1)S(1)}, u32[]{:S(2)}, u32[]{:S(2)}) async-start(bf16[128,2,1296]{2,1,0:T(2,128)(2,1)} %reshape.132), calls=%async_computation.6 | async-start | bytes 1441792 | tf_op jit(solution)/shard_map/all_to_all | solution.py:15
  276.6 2.9 copy-start.3
  276.6 2.9 copy-start.7
